TPU v7x, 32 devices: a whole 2x2x4 slice. The times are simulated.
32 devices in a mesh: stream: 8 (over z, x), span: 4 (over y, core).
Axes of the slice: x: 2, y: 2, z: 4, core: 2. Of those that a mesh axis runs over, the one named last changes fastest.
Arguments:
- positions: float32 [64, 16, 3, 128], P('stream', 'span'), as said below
- velocities: float32 [64, 16, 3, 128], P('stream', 'span'), may hold values from -3 to 3
- strength: float32 [64, 16, 128], P('stream', 'span'), may hold values from 0.5 to 2
- noise: float32 [64, 16, 4, 128], P('stream', 'span'), may hold values from -4 to 4
- counts: int32 [64, 16], P('stream', 'span'), may hold values from 32 to 128
- wall_beads: float32 [64, 16, 3, 128], P('stream', 'span'), as said below
- wall_strength: float32 [64, 16, 128], P('stream', 'span'), may hold values from 0.5 to 2
- wall_faces: int32 [64, 16], P('stream', 'span'), may hold values from 0 to 8
Outputs:
- final_positions: float32 [64, 16, 3, 128], P('stream', 'span')
- final_velocities: float32 [64, 16, 3, 128], P('stream', 'span')
Inputs may be any that keep to these rules, and one draw needn't show every extreme that they name: `positions`: bead i of every cell lies within 0.3 in x and y and within 0.06 in z of the point ((i mod 2) + 0.5, (floor(i / 2) mod 2) + 0.5, (floor(i / 4) + 0.5) / 3). `wall_beads`: wall bead offsets lie in [0, 2) in x and y and in [0, 32/3) in z.
All inputs are finite; a program needn't handle non-finite values.
Results may differ from a plain program's by a relative error of at most 0.0003.
Values sent between devices are 32-bit elements; how exact they have to be, the bound alone decides.
A program may use at most 64 MiB of HBM per device.

v0:
```python
import math

import jax
import jax.numpy as jnp
from jax import lax
from jax.sharding import PartitionSpec as P

STEPS = 3


height = 32.0 / 3.0
cell_side = 2.0
soften = 0.01
repulse = 25.0
friction = 4.5
kick = 3.0
time_step = 0.01


def padded_2(cells, sides, width):
    for axis, dim in sides:
        count = lax.axis_size(axis)
        head = lax.slice_in_dim(cells, 0, width, axis=dim)
        tail = lax.slice_in_dim(cells, cells.shape[dim] - width, cells.shape[dim], axis=dim)
        cells = jnp.concatenate(
            [
                lax.ppermute(tail, axis, [(i, (i + 1) % count) for i in range(count)]),
                cells,
                lax.ppermute(head, axis, [((i + 1) % count, i) for i in range(count)]),
            ],
            axis=dim,
        )
    return cells


def tile_force(own_cells, near_cells, shift_x, shift_y):
    delta_x = own_cells[:, 0, :, None] - (near_cells[:, 0, None, :] + shift_x)
    delta_y = own_cells[:, 1, :, None] - (near_cells[:, 1, None, :] + shift_y)
    delta_z = own_cells[:, 2, :, None] - near_cells[:, 2, None, :]
    delta_z = delta_z - height * jnp.floor(delta_z / height + 0.5)
    dist = jnp.sqrt(delta_x * delta_x + delta_y * delta_y + delta_z * delta_z + soften)
    weight = jnp.maximum(1.0 - dist, 0.0)
    rel_x = own_cells[:, 3, :, None] - near_cells[:, 3, None, :]
    rel_y = own_cells[:, 4, :, None] - near_cells[:, 4, None, :]
    rel_z = own_cells[:, 5, :, None] - near_cells[:, 5, None, :]
    project = (delta_x * rel_x + delta_y * rel_y + delta_z * rel_z) / dist
    alive = own_cells[:, 8, :, None] * near_cells[:, 8, None, :]
    repel = repulse * jnp.sqrt(own_cells[:, 6, :, None] * near_cells[:, 6, None, :])
    theta = (own_cells[:, 7, :, None] + near_cells[:, 7, None, :]) * math.sqrt(0.5)
    coeff = (
        alive
        * weight
        * (repel - friction * weight * project + kick * theta / math.sqrt(time_step))
        / dist
    )
    return jnp.stack(
        [
            jnp.sum(coeff * delta_x, axis=-1),
            jnp.sum(coeff * delta_y, axis=-1),
            jnp.sum(coeff * delta_z, axis=-1),
        ],
        axis=1,
    )


def wall_force(own_cells, wall_cells, facing):
    delta_x = own_cells[:, 0, :, None] - wall_cells[:, 0, None, :]
    delta_y = own_cells[:, 1, :, None] - wall_cells[:, 1, None, :]
    delta_z = own_cells[:, 2, :, None] - wall_cells[:, 2, None, :]
    delta_z = delta_z - height * jnp.floor(delta_z / height + 0.5)
    dist = jnp.sqrt(delta_x * delta_x + delta_y * delta_y + delta_z * delta_z + soften)
    weight = jnp.maximum(1.0 - dist, 0.0)
    project = (
        delta_x * own_cells[:, 3, :, None]
        + delta_y * own_cells[:, 4, :, None]
        + delta_z * own_cells[:, 5, :, None]
    ) / dist
    repel = repulse * jnp.sqrt(own_cells[:, 6, :, None] * wall_cells[:, 3, None, :])
    coeff = (
        facing[:, None, None]
        * own_cells[:, 8, :, None]
        * weight
        * (repel - friction * weight * project)
        / dist
    )
    return jnp.stack(
        [
            jnp.sum(coeff * delta_x, axis=-1),
            jnp.sum(coeff * delta_y, axis=-1),
            jnp.sum(coeff * delta_z, axis=-1),
        ],
        axis=1,
    )


def extend(packed):
    return padded_2(packed, (("stream", 0), ("span", 1)), 1)


def forces(place, speed, strength, noise_row, live, wall_padded):
    packed = jnp.concatenate(
        [place, speed, strength[:, :, None, :], noise_row[:, :, None, :], live[:, :, None, :]],
        axis=2,
    )
    padded = extend(packed)
    rows_here = packed.shape[0]
    cols_here = packed.shape[1]
    slots = packed.shape[-1]
    own_cells = packed.reshape(rows_here * cols_here, 9, slots)
    total = jnp.zeros((rows_here * cols_here, 3, slots), place.dtype)
    for across in (-1, 0, 1):
        for along in (-1, 0, 1):
            near_cells = padded[
                1 + across : 1 + across + rows_here, 1 + along : 1 + along + cols_here
            ]
            near_cells = near_cells.reshape(rows_here * cols_here, 9, slots)
            total = total + tile_force(own_cells, near_cells, across * cell_side, along * cell_side)
            near_walls = wall_padded[
                1 + across : 1 + across + rows_here, 1 + along : 1 + along + cols_here
            ]
            near_walls = near_walls.reshape(rows_here * cols_here, 5, slots)
            wanted = float((1 - across) * 3 + (1 - along))
            facing = (near_walls[:, 4, 0] == wanted).astype(place.dtype)
            total = total + wall_force(own_cells, near_walls, facing)
    return total.reshape(rows_here, cols_here, 3, slots)


def local(positions, velocities, strength, noise, counts, wall_beads, wall_strength, wall_faces):
    slots = jnp.arange(positions.shape[-1], dtype=jnp.int32)
    live = (slots[None, None, :] < counts[:, :, None]).astype(positions.dtype)
    face_row = jnp.broadcast_to(
        wall_faces.astype(positions.dtype)[:, :, None, None],
        (positions.shape[0], positions.shape[1], 1, positions.shape[-1]),
    )
    walls = jnp.concatenate([wall_beads, wall_strength[:, :, None, :], face_row], axis=2)
    wall_padded = padded_2(walls, (("stream", 0), ("span", 1)), 1)
    place, speed = (positions, velocities)
    force = forces(place, speed, strength, noise[:, :, 0, :], live, wall_padded)
    for step in range(STEPS):
        half = speed + 0.5 * time_step * force
        place = place + time_step * half
        force = forces(place, half, strength, noise[:, :, step + 1, :], live, wall_padded)
        speed = half + 0.5 * time_step * force
    return (place, speed)


def solution(mesh):
    in_specs = (
        P("stream", "span", None, None),
        P("stream", "span", None, None),
        P("stream", "span", None),
        P("stream", "span", None, None),
        P("stream", "span"),
        P("stream", "span", None, None),
        P("stream", "span", None),
        P("stream", "span"),
    )
    out_specs = (P("stream", "span", None, None), P("stream", "span", None, None))
    return jax.shard_map(local, mesh=mesh, in_specs=in_specs, out_specs=out_specs, check_vma=False)
```

profile of v0, /device:TPU:0, one launch (start us, length us, event | category | flops | bytes accessed | tf_op | source)
XLA Modules:
  0.0 558.7 jit_solution(13673222269448460113)
XLA Ops:
  40.9 11.4 %fusion.1194 = (f32[32,128]{1,0:T(8,128)S(1)}, f32[32,128]{1,0:T(8,128)S(1)}, f32[32,128]{1,0:T(8,128)S(1)}, f32[32,128]{1,0:T(8,128)S(1)}, f32[32,128]{1,0:T(8,128)S(1)}, /*index=5*/f32[32,128]{1,0:T(8,128)S(1)}) fusion(f32[32,128]{1,0:T(8,128)S(1)} %get-tuple-element.636, f32[32,128]{1,0:T(8,128)S(1)} %get-tuple-element.716, ...), kind=kLoop, calls=%fused_computation.1774 | loop fusion | flops 37724160 | bytes 376832 | tf_op jit(solution)/shard_map/reduce_sum | solution.py:88
  52.3 11.4 %fusion.1226 = (f32[32,128]{1,0:T(8,128)S(1)}, f32[32,128]{1,0:T(8,128)S(1)}, f32[32,128]{1,0:T(8,128)S(1)}, f32[32,128]{1,0:T(8,128)S(1)}, f32[32,128]{1,0:T(8,128)S(1)}, /*index=5*/f32[32,128]{1,0:T(8,128)S(1)}) fusion(f32[32,128]{1,0:T(8,128)S(1)} %get-tuple-element.689, f32[32,128]{1,0:T(8,128)S(1)} %get-tuple-element.716, ...), kind=kLoop, calls=%fused_computation.1806 | loop fusion | flops 37724160 | bytes 376832 | tf_op jit(solution)/shard_map/reduce_sum | solution.py:88
  63.7 11.4 %fusion.1218 = (f32[32,128]{1,0:T(8,128)S(1)}, f32[32,128]{1,0:T(8,128)S(1)}, f32[32,128]{1,0:T(8,128)S(1)}, f32[32,128]{1,0:T(8,128)S(1)}, f32[32,128]{1,0:T(8,128)S(1)}, /*index=5*/f32[32,128]{1,0:T(8,128)S(1)}) fusion(f32[32,128]{1,0:T(8,128)S(1)} %get-tuple-element.654, f32[32,128]{1,0:T(8,128)S(1)} %get-tuple-element.716, ...), kind=kLoop, calls=%fused_computation.1798 | loop fusion | flops 37724160 | bytes 376832 | tf_op jit(solution)/shard_map/reduce_sum | solution.py:88
  75.1 11.4 %fusion.1202 = (f32[32,128]{1,0:T(8,128)S(1)}, f32[32,128]{1,0:T(8,128)S(1)}, f32[32,128]{1,0:T(8,128)S(1)}, f32[32,128]{1,0:T(8,128)S(1)}, f32[32,128]{1,0:T(8,128)S(1)}, /*index=5*/f32[32,128]{1,0:T(8,128)S(1)}) fusion(f32[32,128]{1,0:T(8,128)S(1)} %get-tuple-element.664, f32[32,128]{1,0:T(8,128)S(1)} %get-tuple-element.716, ...), kind=kLoop, calls=%fused_computation.1782 | loop fusion | flops 37724160 | bytes 376832 | tf_op jit(solution)/shard_map/reduce_sum | solution.py:88
  103.0 9.0 %fusion.1214 = (f32[32,128]{1,0:T(8,128)S(1)}, f32[32,128]{1,0:T(8,128)S(1)}, f32[32,128]{1,0:T(8,128)S(1)}) fusion(f32[32,128]{1,0:T(8,128)S(1)} %get-tuple-element.577, f32[32,128]{1,0:T(8,128)S(1)} %get-tuple-element.716, f32[32,128]{1,0:T(8,128)S(1)} %get-tuple-element.570, f32[32,128]{1,0:T(8,128)S(1)} %bitcast.1560, ...), kind=kLoop, calls=%fused_computation.1794 | loop fusion | flops 22532096 | bytes 344064 | tf_op jit(solution)/shard_map/reduce_sum | solution.py:58
  112.0 13.7 %fusion.1190 = (f32[32,128]{1,0:T(8,128)S(1)}, f32[32,128]{1,0:T(8,128)S(1)}, f32[32,128]{1,0:T(8,128)S(1)}, f32[32,128]{1,0:T(8,128)S(1)}, f32[32,128]{1,0:T(8,128)S(1)}, /*index=5*/f32[32,128]{1,0:T(8,128)S(1)}) fusion(f32[32,128]{1,0:T(8,128)S(1)} %get-tuple-element.586, f32[32,128]{1,0:T(8,128)S(1)} %get-tuple-element.716, ...), kind=kLoop, calls=%fused_computation.1770 | loop fusion | flops 45064192 | bytes 393216 | tf_op jit(solution)/shard_map/reduce_sum | solution.py:58
  125.7 8.7 %fusion.1230 = (f32[32,128]{1,0:T(8,128)S(1)}, f32[32,128]{1,0:T(8,128)S(1)}, f32[32,128]{1,0:T(8,128)S(1)}) fusion(f32[32,128]{1,0:T(8,128)S(1)} %get-tuple-element.595, f32[32,128]{1,0:T(8,128)S(1)} %get-tuple-element.716, f32[32,128]{1,0:T(8,128)S(1)} %get-tuple-element.588, f32[32,128]{1,0:T(8,128)S(1)} %bitcast.1562, ...), kind=kLoop, calls=%fused_computation.1810 | loop fusion | flops 22532096 | bytes 344064 | tf_op jit(solution)/shard_map/reduce_sum | solution.py:58
  152.0 11.4 %fusion.1266 = (f32[32,128]{1,0:T(8,128)S(1)}, f32[32,128]{1,0:T(8,128)S(1)}, f32[32,128]{1,0:T(8,128)S(1)}, f32[32,128]{1,0:T(8,128)S(1)}, f32[32,128]{1,0:T(8,128)S(1)}, /*index=5*/f32[32,128]{1,0:T(8,128)S(1)}) fusion(f32[32,128]{1,0:T(8,128)S(1)} %get-tuple-element.683, f32[32,128]{1,0:T(8,128)S(1)} %get-tuple-element.636, ...), kind=kLoop, calls=%fused_computation.1846 | loop fusion | flops 37724160 | bytes 376832 | tf_op jit(solution)/shard_map/reduce_sum | solution.py:88
  163.4 11.4 %fusion.1298 = (f32[32,128]{1,0:T(8,128)S(1)}, f32[32,128]{1,0:T(8,128)S(1)}, f32[32,128]{1,0:T(8,128)S(1)}, f32[32,128]{1,0:T(8,128)S(1)}, f32[32,128]{1,0:T(8,128)S(1)}, /*index=5*/f32[32,128]{1,0:T(8,128)S(1)}) fusion(f32[32,128]{1,0:T(8,128)S(1)} %get-tuple-element.683, f32[32,128]{1,0:T(8,128)S(1)} %get-tuple-element.689, ...), kind=kLoop, calls=%fused_computation.1878 | loop fusion | flops 37724160 | bytes 376832 | tf_op jit(solution)/shard_map/reduce_sum | solution.py:88
  174.8 11.4 %fusion.1290 = (f32[32,128]{1,0:T(8,128)S(1)}, f32[32,128]{1,0:T(8,128)S(1)}, f32[32,128]{1,0:T(8,128)S(1)}, f32[32,128]{1,0:T(8,128)S(1)}, f32[32,128]{1,0:T(8,128)S(1)}, /*index=5*/f32[32,128]{1,0:T(8,128)S(1)}) fusion(f32[32,128]{1,0:T(8,128)S(1)} %get-tuple-element.683, f32[32,128]{1,0:T(8,128)S(1)} %get-tuple-element.654, ...), kind=kLoop, calls=%fused_computation.1870 | loop fusion | flops 37724160 | bytes 376832 | tf_op jit(solution)/shard_map/reduce_sum | solution.py:88
  186.1 11.4 %fusion.1274 = (f32[32,128]{1,0:T(8,128)S(1)}, f32[32,128]{1,0:T(8,128)S(1)}, f32[32,128]{1,0:T(8,128)S(1)}, f32[32,128]{1,0:T(8,128)S(1)}, f32[32,128]{1,0:T(8,128)S(1)}, /*index=5*/f32[32,128]{1,0:T(8,128)S(1)}) fusion(f32[32,128]{1,0:T(8,128)S(1)} %get-tuple-element.683, f32[32,128]{1,0:T(8,128)S(1)} %get-tuple-element.664, ...), kind=kLoop, calls=%fused_computation.1854 | loop fusion | flops 37724160 | bytes 376832 | tf_op jit(solution)/shard_map/reduce_sum | solution.py:88
  211.8 8.8 %fusion.1270 = (f32[32,128]{1,0:T(8,128)S(1)}, f32[32,128]{1,0:T(8,128)S(1)}, f32[32,128]{1,0:T(8,128)S(1)}) fusion(f32[32,128]{1,0:T(8,128)S(1)} %get-tuple-element.481, f32[32,128]{1,0:T(8,128)S(1)} %get-tuple-element.683, f32[32,128]{1,0:T(8,128)S(1)} %get-tuple-element.474, f32[32,128]{1,0:T(8,128)S(1)} %bitcast.1548, ...), kind=kLoop, calls=%fused_computation.1850 | loop fusion | flops 22532096 | bytes 344064 | tf_op jit(solution)/shard_map/reduce_sum | solution.py:58
  220.6 8.7 %fusion.1318 = (f32[32,128]{1,0:T(8,128)S(1)}, f32[32,128]{1,0:T(8,128)S(1)}, f32[32,128]{1,0:T(8,128)S(1)}) fusion(f32[32,128]{1,0:T(8,128)S(1)} %get-tuple-element.537, f32[32,128]{1,0:T(8,128)S(1)} %get-tuple-element.683, f32[32,128]{1,0:T(8,128)S(1)} %get-tuple-element.530, f32[32,128]{1,0:T(8,128)S(1)} %bitcast.1549, ...), kind=kLoop, calls=%fused_computation.1898 | loop fusion | flops 22532096 | bytes 344064 | tf_op jit(solution)/shard_map/reduce_sum | solution.py:58
  247.3 13.7 %fusion.1262 = (f32[32,128]{1,0:T(8,128)S(1)}, f32[32,128]{1,0:T(8,128)S(1)}, f32[32,128]{1,0:T(8,128)S(1)}, f32[32,128]{1,0:T(8,128)S(1)}, f32[32,128]{1,0:T(8,128)S(1)}, /*index=5*/f32[32,128]{1,0:T(8,128)S(1)}) fusion(f32[32,128]{1,0:T(8,128)S(1)} %get-tuple-element.510, f32[32,128]{1,0:T(8,128)S(1)} %get-tuple-element.683, ...), kind=kLoop, calls=%fused_computation.1842 | loop fusion | flops 45064192 | bytes 393216 | tf_op jit(solution)/shard_map/reduce_sum | solution.py:58
  261.0 8.7 %fusion.1302 = (f32[32,128]{1,0:T(8,128)S(1)}, f32[32,128]{1,0:T(8,128)S(1)}, f32[32,128]{1,0:T(8,128)S(1)}) fusion(f32[32,128]{1,0:T(8,128)S(1)} %get-tuple-element.519, f32[32,128]{1,0:T(8,128)S(1)} %get-tuple-element.683, f32[32,128]{1,0:T(8,128)S(1)} %get-tuple-element.512, f32[32,128]{1,0:T(8,128)S(1)} %bitcast.1553, ...), kind=kLoop, calls=%fused_computation.1882 | loop fusion | flops 22532096 | bytes 344064 | tf_op jit(solution)/shard_map/reduce_sum | solution.py:58
  287.3 11.4 %fusion.1338 = (f32[32,128]{1,0:T(8,128)S(1)}, f32[32,128]{1,0:T(8,128)S(1)}, f32[32,128]{1,0:T(8,128)S(1)}, f32[32,128]{1,0:T(8,128)S(1)}, f32[32,128]{1,0:T(8,128)S(1)}, /*index=5*/f32[32,128]{1,0:T(8,128)S(1)}) fusion(f32[32,128]{1,0:T(8,128)S(1)} %get-tuple-element.677, f32[32,128]{1,0:T(8,128)S(1)} %get-tuple-element.636, ...), kind=kLoop, calls=%fused_computation.1918 | loop fusion | flops 37724160 | bytes 376832 | tf_op jit(solution)/shard_map/reduce_sum | solution.py:88
  298.6 11.8 %fusion.1370 = (f32[32,128]{1,0:T(8,128)S(1)}, f32[32,128]{1,0:T(8,128)S(1)}, f32[32,128]{1,0:T(8,128)S(1)}, f32[32,128]{1,0:T(8,128)S(1)}, f32[32,128]{1,0:T(8,128)S(1)}, /*index=5*/f32[32,128]{1,0:T(8,128)S(1)}) fusion(f32[32,128]{1,0:T(8,128)S(1)} %get-tuple-element.677, f32[32,128]{1,0:T(8,128)S(1)} %get-tuple-element.689, ...), kind=kLoop, calls=%fused_computation.1950 | loop fusion | flops 37724160 | bytes 376832 | tf_op jit(solution)/shard_map/reduce_sum | solution.py:88
  310.4 11.4 %fusion.1362 = (f32[32,128]{1,0:T(8,128)S(1)}, f32[32,128]{1,0:T(8,128)S(1)}, f32[32,128]{1,0:T(8,128)S(1)}, f32[32,128]{1,0:T(8,128)S(1)}, f32[32,128]{1,0:T(8,128)S(1)}, /*index=5*/f32[32,128]{1,0:T(8,128)S(1)}) fusion(f32[32,128]{1,0:T(8,128)S(1)} %get-tuple-element.677, f32[32,128]{1,0:T(8,128)S(1)} %get-tuple-element.654, ...), kind=kLoop, calls=%fused_computation.1942 | loop fusion | flops 37724160 | bytes 376832 | tf_op jit(solution)/shard_map/reduce_sum | solution.py:88
  321.8 11.4 %fusion.1346 = (f32[32,128]{1,0:T(8,128)S(1)}, f32[32,128]{1,0:T(8,128)S(1)}, f32[32,128]{1,0:T(8,128)S(1)}, f32[32,128]{1,0:T(8,128)S(1)}, f32[32,128]{1,0:T(8,128)S(1)}, /*index=5*/f32[32,128]{1,0:T(8,128)S(1)}) fusion(f32[32,128]{1,0:T(8,128)S(1)} %get-tuple-element.677, f32[32,128]{1,0:T(8,128)S(1)} %get-tuple-element.664, ...), kind=kLoop, calls=%fused_computation.1926 | loop fusion | flops 37724160 | bytes 376832 | tf_op jit(solution)/shard_map/reduce_sum | solution.py:88
  347.4 8.7 %fusion.1342 = (f32[32,128]{1,0:T(8,128)S(1)}, f32[32,128]{1,0:T(8,128)S(1)}, f32[32,128]{1,0:T(8,128)S(1)}) fusion(f32[32,128]{1,0:T(8,128)S(1)} %get-tuple-element.405, f32[32,128]{1,0:T(8,128)S(1)} %get-tuple-element.677, f32[32,128]{1,0:T(8,128)S(1)} %get-tuple-element.398, f32[32,128]{1,0:T(8,128)S(1)} %bitcast.1539, ...), kind=kLoop, calls=%fused_computation.1922 | loop fusion | flops 22532096 | bytes 344064 | tf_op jit(solution)/shard_map/reduce_sum | solution.py:58
  365.4 8.7 %fusion.1350 = (f32[32,128]{1,0:T(8,128)S(1)}, f32[32,128]{1,0:T(8,128)S(1)}, f32[32,128]{1,0:T(8,128)S(1)}) fusion(f32[32,128]{1,0:T(8,128)S(1)} %get-tuple-element.416, f32[32,128]{1,0:T(8,128)S(1)} %get-tuple-element.677, f32[32,128]{1,0:T(8,128)S(1)} %get-tuple-element.409, f32[32,128]{1,0:T(8,128)S(1)} %bitcast.1541, ...), kind=kLoop, calls=%fused_computation.1930 | loop fusion | flops 22532096 | bytes 344064 | tf_op jit(solution)/shard_map/reduce_sum | solution.py:58
  374.0 8.7 %fusion.1358 = (f32[32,128]{1,0:T(8,128)S(1)}, f32[32,128]{1,0:T(8,128)S(1)}, f32[32,128]{1,0:T(8,128)S(1)}) fusion(f32[32,128]{1,0:T(8,128)S(1)} %get-tuple-element.425, f32[32,128]{1,0:T(8,128)S(1)} %get-tuple-element.677, f32[32,128]{1,0:T(8,128)S(1)} %get-tuple-element.418, f32[32,128]{1,0:T(8,128)S(1)} %bitcast.1542, ...), kind=kLoop, calls=%fused_computation.1938 | loop fusion | flops 22532096 | bytes 344064 | tf_op jit(solution)/shard_map/reduce_sum | solution.py:58
  382.7 13.7 %fusion.1334 = (f32[32,128]{1,0:T(8,128)S(1)}, f32[32,128]{1,0:T(8,128)S(1)}, f32[32,128]{1,0:T(8,128)S(1)}, f32[32,128]{1,0:T(8,128)S(1)}, f32[32,128]{1,0:T(8,128)S(1)}, /*index=5*/f32[32,128]{1,0:T(8,128)S(1)}) fusion(f32[32,128]{1,0:T(8,128)S(1)} %get-tuple-element.434, f32[32,128]{1,0:T(8,128)S(1)} %get-tuple-element.677, ...), kind=kLoop, calls=%fused_computation.1914 | loop fusion | flops 45064192 | bytes 393216 | tf_op jit(solution)/shard_map/reduce_sum | solution.py:58
  396.4 8.7 %fusion.1374 = (f32[32,128]{1,0:T(8,128)S(1)}, f32[32,128]{1,0:T(8,128)S(1)}, f32[32,128]{1,0:T(8,128)S(1)}) fusion(f32[32,128]{1,0:T(8,128)S(1)} %get-tuple-element.443, f32[32,128]{1,0:T(8,128)S(1)} %get-tuple-element.677, f32[32,128]{1,0:T(8,128)S(1)} %get-tuple-element.436, f32[32,128]{1,0:T(8,128)S(1)} %bitcast.1544, ...), kind=kLoop, calls=%fused_computation.1954 | loop fusion | flops 22532096 | bytes 344064 | tf_op jit(solution)/shard_map/reduce_sum | solution.py:58
  405.1 8.7 %fusion.1382 = (f32[32,128]{1,0:T(8,128)S(1)}, f32[32,128]{1,0:T(8,128)S(1)}, f32[32,128]{1,0:T(8,128)S(1)}) fusion(f32[32,128]{1,0:T(8,128)S(1)} %get-tuple-element.452, f32[32,128]{1,0:T(8,128)S(1)} %get-tuple-element.677, f32[32,128]{1,0:T(8,128)S(1)} %get-tuple-element.445, f32[32,128]{1,0:T(8,128)S(1)} %bitcast.1545, ...), kind=kLoop, calls=%fused_computation.1962 | loop fusion | flops 22532096 | bytes 344064 | tf_op jit(solution)/shard_map/reduce_sum | solution.py:58
  413.8 8.7 %fusion.1398 = (f32[32,128]{1,0:T(8,128)S(1)}, f32[32,128]{1,0:T(8,128)S(1)}, f32[32,128]{1,0:T(8,128)S(1)}) fusion(f32[32,128]{1,0:T(8,128)S(1)} %get-tuple-element.470, f32[32,128]{1,0:T(8,128)S(1)} %get-tuple-element.677, f32[32,128]{1,0:T(8,128)S(1)} %get-tuple-element.463, f32[32,128]{1,0:T(8,128)S(1)} %bitcast.1546, ...), kind=kLoop, calls=%fused_computation.1978 | loop fusion | flops 22532096 | bytes 344064 | tf_op jit(solution)/shard_map/reduce_sum | solution.py:58
  422.7 11.4 %fusion.1410 = (f32[32,128]{1,0:T(8,128)S(1)}, f32[32,128]{1,0:T(8,128)S(1)}, f32[32,128]{1,0:T(8,128)S(1)}, f32[32,128]{1,0:T(8,128)S(1)}, f32[32,128]{1,0:T(8,128)S(1)}, /*index=5*/f32[32,128]{1,0:T(8,128)S(1)}) fusion(f32[32,128]{1,0:T(8,128)S(1)} %get-tuple-element.671, f32[32,128]{1,0:T(8,128)S(1)} %get-tuple-element.636, ...), kind=kLoop, calls=%fused_computation.1990 | loop fusion | flops 37724160 | bytes 376832 | tf_op jit(solution)/shard_map/reduce_sum | solution.py:88
  434.1 11.5 %fusion.1418 = (f32[32,128]{1,0:T(8,128)S(1)}, f32[32,128]{1,0:T(8,128)S(1)}, f32[32,128]{1,0:T(8,128)S(1)}, f32[32,128]{1,0:T(8,128)S(1)}, f32[32,128]{1,0:T(8,128)S(1)}, /*index=5*/f32[32,128]{1,0:T(8,128)S(1)}) fusion(f32[32,128]{1,0:T(8,128)S(1)} %get-tuple-element.671, f32[32,128]{1,0:T(8,128)S(1)} %get-tuple-element.664, ...), kind=kLoop, calls=%fused_computation.1998 | loop fusion | flops 37724160 | bytes 376832 | tf_op jit(solution)/shard_map/reduce_sum | solution.py:88
  445.6 11.4 %fusion.1434 = (f32[32,128]{1,0:T(8,128)S(1)}, f32[32,128]{1,0:T(8,128)S(1)}, f32[32,128]{1,0:T(8,128)S(1)}, f32[32,128]{1,0:T(8,128)S(1)}, f32[32,128]{1,0:T(8,128)S(1)}, /*index=5*/f32[32,128]{1,0:T(8,128)S(1)}) fusion(f32[32,128]{1,0:T(8,128)S(1)} %get-tuple-element.671, f32[32,128]{1,0:T(8,128)S(1)} %get-tuple-element.654, ...), kind=kLoop, calls=%fused_computation.2014 | loop fusion | flops 37724160 | bytes 376832 | tf_op jit(solution)/shard_map/reduce_sum | solution.py:88
  457.0 11.4 %fusion.1442 = (f32[32,128]{1,0:T(8,128)S(1)}, f32[32,128]{1,0:T(8,128)S(1)}, f32[32,128]{1,0:T(8,128)S(1)}, f32[32,128]{1,0:T(8,128)S(1)}, f32[32,128]{1,0:T(8,128)S(1)}, /*index=5*/f32[32,128]{1,0:T(8,128)S(1)}) fusion(f32[32,128]{1,0:T(8,128)S(1)} %get-tuple-element.671, f32[32,128]{1,0:T(8,128)S(1)} %get-tuple-element.689, ...), kind=kLoop, calls=%fused_computation.2022 | loop fusion | flops 37724160 | bytes 376832 | tf_op jit(solution)/shard_map/reduce_sum | solution.py:88
  482.6 8.7 %fusion.1414 = (f32[32,128]{1,0:T(8,128)S(1)}, f32[32,128]{1,0:T(8,128)S(1)}, f32[32,128]{1,0:T(8,128)S(1)}) fusion(f32[32,128]{1,0:T(8,128)S(1)} %get-tuple-element.329, f32[32,128]{1,0:T(8,128)S(1)} %get-tuple-element.671, f32[32,128]{1,0:T(8,128)S(1)} %get-tuple-element.322, f32[32,128]{1,0:T(8,128)S(1)} %bitcast.1530, ...), kind=kLoop, calls=%fused_computation.1994 | loop fusion | flops 22532096 | bytes 344064 | tf_op jit(solution)/shard_map/reduce_sum | solution.py:58
  517.9 13.7 %fusion.1406 = (f32[32,128]{1,0:T(8,128)S(1)}, f32[32,128]{1,0:T(8,128)S(1)}, f32[32,128]{1,0:T(8,128)S(1)}, f32[32,128]{1,0:T(8,128)S(1)}, f32[32,128]{1,0:T(8,128)S(1)}, /*index=5*/f32[32,128]{1,0:T(8,128)S(1)}) fusion(f32[32,128]{1,0:T(8,128)S(1)} %get-tuple-element.358, f32[32,128]{1,0:T(8,128)S(1)} %get-tuple-element.671, ...), kind=kLoop, calls=%fused_computation.1986 | loop fusion | flops 45064192 | bytes 393216 | tf_op jit(solution)/shard_map/reduce_sum | solution.py:58
  (237 shorter events, 214.4 us)
Async XLA Ops:
  0.6 10.4 %copy-start.6 = (s32[8,4]{0,1:T(4,128)S(1)}, s32[8,4]{0,1:T(4,128)}, u32[]{:S(2)}) copy-start(s32[8,4]{0,1:T(4,128)} %param.15) | copy-start | bytes 388
  0.6 10.6 %copy-start.3 = (f32[8,4,128]{2,1,0:T(4,128)S(1)}, f32[8,4,128]{2,1,0:T(4,128)}, u32[]{:S(2)}) copy-start(f32[8,4,128]{2,1,0:T(4,128)} %param.14) | copy-start | bytes 49156
  0.7 10.6 %copy-start = (f32[8,4,3,128]{3,1,2,0:T(4,128)S(1)}, f32[8,4,3,128]{3,1,2,0:T(4,128)}, u32[]{:S(2)}) copy-start(f32[8,4,3,128]{3,1,2,0:T(4,128)} %param.13) | copy-start | bytes 147460
  1.7 14.5 %copy-start.2 = (f32[8,4,3,128]{3,1,2,0:T(4,128)S(1)}, f32[8,4,3,128]{3,1,2,0:T(4,128)}, u32[]{:S(2)}) copy-start(f32[8,4,3,128]{3,1,2,0:T(4,128)} %param.9) | copy-start | bytes 147460
  2.5 13.7 %copy-start.1 = (f32[8,4,3,128]{3,1,2,0:T(4,128)S(1)}, f32[8,4,3,128]{3,1,2,0:T(4,128)}, u32[]{:S(2)}) copy-start(f32[8,4,3,128]{3,1,2,0:T(4,128)} %param.8) | copy-start | bytes 147460
  5.0 14.8 %collective-permute-start = (f32[1,4,9,128]{3,1,2,0:T(4,128)S(1)}, f32[1,4,9,128]{3,1,2,0:T(4,128)S(1)}, u32[]{:S(2)}, u32[]{:S(2)}) collective-permute-start(f32[1,4,9,128]{3,1,2,0:T(4,128)S(1)} %get-tuple-element.623), channel_id=1, source_target_pairs={{0,4},{4,8},{8,12},{12,16},{16,20},{20,24},{24,28},{28,0},{1,5},{5... | collective-permute-start | bytes 55304 | tf_op jit(solution)/shard_map/ppermute | solution.py:27
  8.0 11.8 %collective-permute-start.1 = (f32[1,4,9,128]{3,1,2,0:T(4,128)S(1)}, f32[1,4,9,128]{3,1,2,0:T(4,128)S(1)}, u32[]{:S(2)}, u32[]{:S(2)}) collective-permute-start(f32[1,4,9,128]{3,1,2,0:T(4,128)S(1)} %get-tuple-element.624), channel_id=1, source_target_pairs={{4,0},{8,4},{12,8},{16,12},{20,16},{24,20},{28,24},{0,28},{5,1},{9... | collective-permute-start | bytes 55304 | tf_op jit(solution)/shard_map/ppermute | solution.py:29
  11.2 6.4 %collective-permute-start.3 = (f32[1,4,5,128]{3,1,2,0:T(4,128)S(1)}, f32[1,4,5,128]{3,1,2,0:T(4,128)S(1)}, u32[]{:S(2)}, u32[]{:S(2)}) collective-permute-start(f32[1,4,5,128]{3,1,2,0:T(4,128)S(1)} %get-tuple-element.660), channel_id=1, source_target_pairs={{0,4},{4,8},{8,12},{12,16},{16,20},{20,24},{24,28},{28,0},{1,5},{5... | collective-permute-start | bytes 30728 | tf_op jit(solution)/shard_map/ppermute | solution.py:27
  11.3 6.4 %collective-permute-start.4 = (f32[1,4,5,128]{3,1,2,0:T(4,128)S(1)}, f32[1,4,5,128]{3,1,2,0:T(4,128)S(1)}, u32[]{:S(2)}, u32[]{:S(2)}) collective-permute-start(f32[1,4,5,128]{3,1,2,0:T(4,128)S(1)} %get-tuple-element.659), channel_id=1, source_target_pairs={{4,0},{8,4},{12,8},{16,12},{20,16},{24,20},{28,24},{0,28},{5,1},{9... | collective-permute-start | bytes 30728 | tf_op jit(solution)/shard_map/ppermute | solution.py:29
  18.0 21.8 %collective-permute-start.5 = (f32[10,1,5,128]{3,1,2,0:T(1,128)S(1)}, f32[10,1,5,128]{3,1,2,0:T(1,128)S(1)}, u32[]{:S(2)}, u32[]{:S(2)}) collective-permute-start(f32[10,1,5,128]{3,1,2,0:T(1,128)S(1)} %get-tuple-element.627), channel_id=1, source_target_pairs={{0,1},{1,2},{2,3},{3,0},{4,5},{5,6},{6,7},{7,4},{8,9},{9,10},{10,1... | collective-permute-start | bytes 76808 | tf_op jit(solution)/shard_map/ppermute | solution.py:27
  18.0 21.8 %collective-permute-start.7 = (f32[10,1,5,128]{3,1,2,0:T(1,128)S(1)}, f32[10,1,5,128]{3,1,2,0:T(1,128)S(1)}, u32[]{:S(2)}, u32[]{:S(2)}) collective-permute-start(f32[10,1,5,128]{3,1,2,0:T(1,128)S(1)} %get-tuple-element.628), channel_id=1, source_target_pairs={{1,0},{2,1},{3,2},{0,3},{5,4},{6,5},{7,6},{4,7},{9,8},{10,9},{11,1... | collective-permute-start | bytes 76808 | tf_op jit(solution)/shard_map/ppermute | solution.py:29
  19.8 73.9 %collective-permute-start.2 = (f32[10,1,9,128]{3,1,2,0:T(1,128)S(1)}, f32[10,1,9,128]{3,1,2,0:T(1,128)S(1)}, u32[]{:S(2)}, u32[]{:S(2)}) collective-permute-start(f32[10,1,9,128]{3,1,2,0:T(1,128)S(1)} %get-tuple-element.319), channel_id=1, source_target_pairs={{0,1},{1,2},{2,3},{3,0},{4,5},{5,6},{6,7},{7,4},{8,9},{9,10},{10,1... | collective-permute-start | bytes 138248 | tf_op jit(solution)/shard_map/ppermute | solution.py:27
  19.9 73.8 %collective-permute-start.6 = (f32[10,1,9,128]{3,1,2,0:T(1,128)S(1)}, f32[10,1,9,128]{3,1,2,0:T(1,128)S(1)}, u32[]{:S(2)}, u32[]{:S(2)}) collective-permute-start(f32[10,1,9,128]{3,1,2,0:T(1,128)S(1)} %get-tuple-element.320), channel_id=1, source_target_pairs={{1,0},{2,1},{3,2},{0,3},{5,4},{6,5},{7,6},{4,7},{9,8},{10,9},{11,1... | collective-permute-start | bytes 138248 | tf_op jit(solution)/shard_map/ppermute | solution.py:29
  21.7 0.7 copy-start.4
  197.7 12.1 %collective-permute-start.8 = (f32[1,4,9,128]{3,1,2,0:T(4,128)S(1)}, f32[1,4,9,128]{3,1,2,0:T(4,128)S(1)}, u32[]{:S(2)}, u32[]{:S(2)}) collective-permute-start(f32[1,4,9,128]{3,1,2,0:T(4,128)S(1)} %get-tuple-element.547), channel_id=1, source_target_pairs={{0,4},{4,8},{8,12},{12,16},{16,20},{20,24},{24,28},{28,0},{1,5},{5... | collective-permute-start | bytes 55304 | tf_op jit(solution)/shard_map/ppermute | solution.py:27
  197.7 12.0 %collective-permute-start.9 = (f32[1,4,9,128]{3,1,2,0:T(4,128)S(1)}, f32[1,4,9,128]{3,1,2,0:T(4,128)S(1)}, u32[]{:S(2)}, u32[]{:S(2)}) collective-permute-start(f32[1,4,9,128]{3,1,2,0:T(4,128)S(1)} %get-tuple-element.548), channel_id=1, source_target_pairs={{4,0},{8,4},{12,8},{16,12},{20,16},{24,20},{28,24},{0,28},{5,1},{9... | collective-permute-start | bytes 55304 | tf_op jit(solution)/shard_map/ppermute | solution.py:29
  209.9 19.4 %collective-permute-start.10 = (f32[10,1,9,128]{3,1,2,0:T(1,128)S(1)}, f32[10,1,9,128]{3,1,2,0:T(1,128)S(1)}, u32[]{:S(2)}, u32[]{:S(2)}) collective-permute-start(f32[10,1,9,128]{3,1,2,0:T(1,128)S(1)} %get-tuple-element.315), channel_id=1, source_target_pairs={{0,1},{1,2},{2,3},{3,0},{4,5},{5,6},{6,7},{7,4},{8,9},{9,10},{10,1... | collective-permute-start | bytes 138248 | tf_op jit(solution)/shard_map/ppermute | solution.py:27
  210.0 19.3 %collective-permute-start.11 = (f32[10,1,9,128]{3,1,2,0:T(1,128)S(1)}, f32[10,1,9,128]{3,1,2,0:T(1,128)S(1)}, u32[]{:S(2)}, u32[]{:S(2)}) collective-permute-start(f32[10,1,9,128]{3,1,2,0:T(1,128)S(1)} %get-tuple-element.316), channel_id=1, source_target_pairs={{1,0},{2,1},{3,2},{0,3},{5,4},{6,5},{7,6},{4,7},{9,8},{10,9},{11,1... | collective-permute-start | bytes 138248 | tf_op jit(solution)/shard_map/ppermute | solution.py:29
  333.3 12.0 %collective-permute-start.12 = (f32[1,4,9,128]{3,1,2,0:T(4,128)S(1)}, f32[1,4,9,128]{3,1,2,0:T(4,128)S(1)}, u32[]{:S(2)}, u32[]{:S(2)}) collective-permute-start(f32[1,4,9,128]{3,1,2,0:T(4,128)S(1)} %get-tuple-element.471), channel_id=1, source_target_pairs={{0,4},{4,8},{8,12},{12,16},{16,20},{20,24},{24,28},{28,0},{1,5},{5... | collective-permute-start | bytes 55304 | tf_op jit(solution)/shard_map/ppermute | solution.py:27
  333.4 11.9 %collective-permute-start.13 = (f32[1,4,9,128]{3,1,2,0:T(4,128)S(1)}, f32[1,4,9,128]{3,1,2,0:T(4,128)S(1)}, u32[]{:S(2)}, u32[]{:S(2)}) collective-permute-start(f32[1,4,9,128]{3,1,2,0:T(4,128)S(1)} %get-tuple-element.472), channel_id=1, source_target_pairs={{4,0},{8,4},{12,8},{16,12},{20,16},{24,20},{28,24},{0,28},{5,1},{9... | collective-permute-start | bytes 55304 | tf_op jit(solution)/shard_map/ppermute | solution.py:29
  345.5 19.2 %collective-permute-start.14 = (f32[10,1,9,128]{3,1,2,0:T(1,128)S(1)}, f32[10,1,9,128]{3,1,2,0:T(1,128)S(1)}, u32[]{:S(2)}, u32[]{:S(2)}) collective-permute-start(f32[10,1,9,128]{3,1,2,0:T(1,128)S(1)} %get-tuple-element.311), channel_id=1, source_target_pairs={{0,1},{1,2},{2,3},{3,0},{4,5},{5,6},{6,7},{7,4},{8,9},{9,10},{10,1... | collective-permute-start | bytes 138248 | tf_op jit(solution)/shard_map/ppermute | solution.py:27
  345.6 19.1 %collective-permute-start.15 = (f32[10,1,9,128]{3,1,2,0:T(1,128)S(1)}, f32[10,1,9,128]{3,1,2,0:T(1,128)S(1)}, u32[]{:S(2)}, u32[]{:S(2)}) collective-permute-start(f32[10,1,9,128]{3,1,2,0:T(1,128)S(1)} %get-tuple-element.312), channel_id=1, source_target_pairs={{1,0},{2,1},{3,2},{0,3},{5,4},{6,5},{7,6},{4,7},{9,8},{10,9},{11,1... | collective-permute-start | bytes 138248 | tf_op jit(solution)/shard_map/ppermute | solution.py:29
  422.6 11.5 %copy-start.5 = (f32[8,4,3,128]{3,1,2,0:T(4,128)}, f32[8,4,3,128]{3,1,2,0:T(4,128)S(1)}, u32[]{:S(2)}) copy-start(f32[8,4,3,128]{3,1,2,0:T(4,128)S(1)} %get-tuple-element.267) | copy-start | bytes 147460
  468.5 12.0 %collective-permute-start.16 = (f32[1,4,9,128]{3,1,2,0:T(4,128)S(1)}, f32[1,4,9,128]{3,1,2,0:T(4,128)S(1)}, u32[]{:S(2)}, u32[]{:S(2)}) collective-permute-start(f32[1,4,9,128]{3,1,2,0:T(4,128)S(1)} %get-tuple-element.386), channel_id=1, source_target_pairs={{0,4},{4,8},{8,12},{12,16},{16,20},{20,24},{24,28},{28,0},{1,5},{5... | collective-permute-start | bytes 55304 | tf_op jit(solution)/shard_map/ppermute | solution.py:27
  468.6 11.9 %collective-permute-start.17 = (f32[1,4,9,128]{3,1,2,0:T(4,128)S(1)}, f32[1,4,9,128]{3,1,2,0:T(4,128)S(1)}, u32[]{:S(2)}, u32[]{:S(2)}) collective-permute-start(f32[1,4,9,128]{3,1,2,0:T(4,128)S(1)} %get-tuple-element.387), channel_id=1, source_target_pairs={{4,0},{8,4},{12,8},{16,12},{20,16},{24,20},{28,24},{0,28},{5,1},{9... | collective-permute-start | bytes 55304 | tf_op jit(solution)/shard_map/ppermute | solution.py:29
  480.8 19.2 %collective-permute-start.18 = (f32[10,1,9,128]{3,1,2,0:T(1,128)S(1)}, f32[10,1,9,128]{3,1,2,0:T(1,128)S(1)}, u32[]{:S(2)}, u32[]{:S(2)}) collective-permute-start(f32[10,1,9,128]{3,1,2,0:T(1,128)S(1)} %get-tuple-element.307), channel_id=1, source_target_pairs={{0,1},{1,2},{2,3},{3,0},{4,5},{5,6},{6,7},{7,4},{8,9},{9,10},{10,1... | collective-permute-start | bytes 138248 | tf_op jit(solution)/shard_map/ppermute | solution.py:27
  480.8 19.1 %collective-permute-start.19 = (f32[10,1,9,128]{3,1,2,0:T(1,128)S(1)}, f32[10,1,9,128]{3,1,2,0:T(1,128)S(1)}, u32[]{:S(2)}, u32[]{:S(2)}) collective-permute-start(f32[10,1,9,128]{3,1,2,0:T(1,128)S(1)} %get-tuple-element.308), channel_id=1, source_target_pairs={{1,0},{2,1},{3,2},{0,3},{5,4},{6,5},{7,6},{4,7},{9,8},{10,9},{11,1... | collective-permute-start | bytes 138248 | tf_op jit(solution)/shard_map/ppermute | solution.py:29
where the time goes:
time: 568 us; the launch traced here: 559 us
  other arithmetic  513 us (90%)
  starting transfers between devices  34.2 us (6%)
  local copies, waits for them, and re-layouts  7.19 us (1%)
    reduce_sum x32, other arithmetic, tile_force(): jnp.sum(coeff * delta_x, axis=-1)  298 us
    reduce_sum x20, other arithmetic, wall_force(): jnp.sum(coeff * delta_x, axis=-1)  211 us
    ppermute x10, starting transfers between devices, padded_2(): lax.ppermute(head, axis, [((i + 1) % count, i) for i in range(count)])  30.7 us
  transfers between devices with their start and end apart: 20, of which 1 were waited for; matrix products, arithmetic and copies ran while one was open for 26% of the time, Pallas kernels for 0%

commit v1 on v0

--- a/solution.py
+++ b/solution.py
@@ -3,6 +3,8 @@
 import jax
 import jax.numpy as jnp
 from jax import lax
+from jax.experimental import pallas as pl
+from jax.experimental.pallas import tpu as pltpu
 from jax.sharding import PartitionSpec as P
 
 STEPS = 3
@@ -125,7 +127,7 @@
     return total.reshape(rows_here, cols_here, 3, slots)
 
 
-def local(positions, velocities, strength, noise, counts, wall_beads, wall_strength, wall_faces):
+def every_pair(positions, velocities, strength, noise, counts, wall_beads, wall_strength, wall_faces):
     slots = jnp.arange(positions.shape[-1], dtype=jnp.int32)
     live = (slots[None, None, :] < counts[:, :, None]).astype(positions.dtype)
     face_row = jnp.broadcast_to(
@@ -144,6 +146,345 @@
     return (place, speed)
 
 
+REACH_XY = 0.49
+REACH_Z = 0.33
+FAR = 1.0e4
+OWN = 8
+STATIC = 10
+MESH = pl.DeviceIdType.MESH
+
+
+def lattice(shape):
+    lane = lax.broadcasted_iota(jnp.int32, shape, len(shape) - 1)
+    return lane, (
+        (lane % 2).astype(jnp.float32) + 0.5,
+        (lane // 2 % 2).astype(jnp.float32) + 0.5,
+        ((lane // 4).astype(jnp.float32) + 0.5) * (1.0 / 3.0),
+    )
+
+
+def kernel(
+    counts_ref, faces_ref, pos_ref, vel_ref, str_ref, noise_ref, wall_ref, wstr_ref,
+    out_x, out_v, bad_ref,
+    cells, own, now, live_ref, wide, target, push, near, force, send_sem, recv_sem,
+):
+    tx, ty = lax.axis_size("stream"), lax.axis_size("span")
+    ix, iy = lax.axis_index("stream"), lax.axis_index("span")
+    around = [(p, q) for p in (-1, 0, 1) for q in (-1, 0, 1) if (p, q) != (0, 0)]
+
+    def device(p, q):
+        return (lax.rem(ix + p + tx, tx), lax.rem(iy + q + ty, ty))
+
+    barrier = pltpu.get_barrier_semaphore()
+    for p, q in around:
+        pl.semaphore_signal(barrier, inc=1, device_id=device(p, q), device_id_type=MESH)
+
+    lane, point = lattice((8, 128))
+    lane_row = lax.broadcasted_iota(jnp.int32, (1, 128), 1)
+
+    for cx in range(8):
+        for cy in range(4):
+            row = pl.ds(OWN + cx, 1)
+            live_ref[cy, pl.ds(cx, 1), :] = jnp.where(
+                lane_row < counts_ref[cx, cy], 1.0, 0.0
+            ).astype(jnp.float32)
+            for c in range(3):
+                now[c, cy, pl.ds(cx, 1), :] = pos_ref[cx, cy, pl.ds(c, 1), :]
+                now[3 + c, cy, pl.ds(cx, 1), :] = vel_ref[cx, cy, pl.ds(c, 1), :]
+                cells[5 + c, 1 + cy, row, :] = wall_ref[cx, cy, pl.ds(c, 1), :]
+            for c in range(4):
+                cells[1 + c, 1 + cy, row, :] = noise_ref[cx, cy, pl.ds(c, 1), :] * (
+                    kick * math.sqrt(0.5) / math.sqrt(time_step)
+                )
+            cells[0, 1 + cy, row, :] = 5.0 * jnp.sqrt(str_ref[cx, pl.ds(cy, 1), :])
+            cells[8, 1 + cy, row, :] = 5.0 * jnp.sqrt(wstr_ref[cx, pl.ds(cy, 1), :])
+            cells[9, 1 + cy, row, :] = jnp.zeros((1, 128), jnp.float32) + faces_ref[cx, cy].astype(
+                jnp.float32
+            )
+    own[...] = jnp.full(own.shape, FAR, jnp.float32)
+    for cy in range(4):
+        own[6, cy, pl.ds(OWN, 8), :] = cells[0, 1 + cy, pl.ds(OWN, 8), :]
+    bad_ref[...] = jnp.zeros((8, 128), jnp.float32)
+
+    def edge(p, q, first, count):
+        rows = {-1: (OWN, OWN + 8, 1), 0: (OWN, OWN, 8), 1: (OWN + 7, OWN - 1, 1)}[p]
+        cols = {-1: (1, 5, 1), 0: (1, 1, 4), 1: (4, 0, 1)}[q]
+        comps = pl.ds(first, count)
+        return (
+            cells.at[comps, pl.ds(cols[0], cols[2]), pl.ds(rows[0], rows[2]), :],
+            cells.at[comps, pl.ds(cols[1], cols[2]), pl.ds(rows[1], rows[2]), :],
+        )
+
+    def publish(t):
+        first = STATIC + 6 * t
+        bad = bad_ref[...]
+        for cy in range(4):
+            live = live_ref[cy] > 0.5
+            for c in range(3):
+                offset = now[c, cy] - point[c]
+                limit = REACH_Z if c == 2 else REACH_XY
+                fits = jnp.abs(offset) <= limit
+                bad = jnp.maximum(bad, jnp.where(live, jnp.where(fits, 0.0, 1.0), 0.0))
+                offset = jnp.where(live, offset, FAR)
+                speed = friction * now[3 + c, cy]
+                cells[first + c, 1 + cy, pl.ds(OWN, 8), :] = offset
+                cells[first + 3 + c, 1 + cy, pl.ds(OWN, 8), :] = speed
+                own[c, cy, pl.ds(OWN, 8), :] = offset
+                own[3 + c, cy, pl.ds(OWN, 8), :] = speed
+        bad_ref[...] = bad
+        copies = []
+        for n, (p, q) in enumerate(around):
+            src, dst = edge(p, q, 0 if t == 0 else first, STATIC + 6 if t == 0 else 6)
+            copy = pltpu.make_async_remote_copy(
+                src_ref=src,
+                dst_ref=dst,
+                send_sem=send_sem.at[t, n],
+                recv_sem=recv_sem.at[t, n],
+                device_id=device(p, q),
+                device_id_type=MESH,
+            )
+            copy.start()
+            copies.append(copy)
+        return copies
+
+    def widen(cy, base, rows, block_of):
+        tiles = [cells[5 + c, cy, pl.ds(base, 8), :].T for c in range(4)]
+        for s in rows:
+            block = block_of(s)
+            for c in range(4):
+                for part in range(16):
+                    column = jnp.broadcast_to(tiles[c][8 * part : 8 * part + 8, s : s + 1], (8, 128))
+                    if c < 3:
+                        column = column - point[c]
+                    if c == 2:
+                        column = column - height * jnp.floor(column * (1.0 / height) + 0.5)
+                    wide[block, c, pl.ds(8 * part, 8), :] = column
+
+    def aim(cy, base, rows):
+        face = cells[9, cy, pl.ds(base, 8), :]
+        found = [jnp.full((8, 128), FAR, jnp.float32)] * 3 + [jnp.zeros((8, 128), jnp.float32)] * 4
+        for q in (-1, 0, 1):
+            if not 1 <= cy + q <= 4:
+                continue
+            for p in (-1, 0, 1):
+                if (base < OWN and p != 1) or (base > OWN and p != -1):
+                    continue
+                hit = face == float(3 * (p + 1) + (q + 1))
+                for c in range(7):
+                    found[c] = jnp.where(
+                        hit, own[c, cy + q - 1, pl.ds(base + p, 8), :], found[c]
+                    )
+        for c in range(7):
+            target[c, cy, pl.ds(base, 8), :] = found[c]
+
+    def aim_own():
+        for cy in range(1, 5):
+            aim(cy, OWN, None)
+
+    def aim_ring():
+        for cy in (0, 5):
+            aim(cy, OWN, None)
+        for cy in range(6):
+            aim(cy, OWN - 8, None)
+            aim(cy, OWN + 8, None)
+
+    def wall_block(block, cy, row):
+        at = [
+            jnp.broadcast_to(target[c, cy, pl.ds(row, 1), :], (8, 128)) for c in range(7)
+        ]
+        total = [jnp.zeros((8, 128), jnp.float32) for _ in range(3)]
+        for part in range(16):
+            d = [at[c] - wide[block, c, pl.ds(8 * part, 8), :] for c in range(3)]
+            square = d[0] * d[0] + d[1] * d[1] + (d[2] * d[2] + soften)
+            inverse = lax.rsqrt(square)
+            weight = jnp.maximum(1.0 - square * inverse, 0.0) * inverse
+            dot = d[0] * at[3] + d[1] * at[4] + d[2] * at[5]
+            repel = at[6] * wide[block, 3, pl.ds(8 * part, 8), :]
+            coeff = weight * (repel - weight * dot)
+            total = [total[c] + coeff * d[c] for c in range(3)]
+        for c in range(3):
+            push[c, cy, pl.ds(row, 1), :] = jnp.sum(total[c], axis=0, keepdims=True)
+
+    def walls_rows(low, high):
+        def body(b, carry):
+            wall_block(b, b // 8, OWN + b % 8)
+            return carry
+
+        lax.fori_loop(low, high, body, 0)
+
+    def walls_sides():
+        def body(h, carry):
+            wall_block(48 + h, h % 6, OWN - 1 + 9 * (h // 6))
+            return carry
+
+        lax.fori_loop(0, 12, body, 0)
+
+    def swap(value, step, low):
+        return jnp.where(low, pltpu.roll(value, 128 - step, 1), pltpu.roll(value, step, 1))
+
+    low_x = lane % 2 == 0
+    low_y = lane // 2 % 2 == 0
+
+    def gather_near(t):
+        def body(c, carry):
+            comp = jnp.where(c < 6, STATIC + 6 * t + c, jnp.where(c == 6, 0, 1 + t))
+            is_x = jnp.where(c == 0, 1.0, 0.0)
+            is_y = jnp.where(c == 1, 1.0, 0.0)
+            along_x = {-1: [], 0: [], 1: []}
+            for cy in range(6):
+                mid = cells[comp, cy, pl.ds(OWN, 8), :]
+                before = cells[comp, cy, pl.ds(OWN - 1, 8), :]
+                after = cells[comp, cy, pl.ds(OWN + 1, 8), :]
+                along_x[0].append(mid)
+                along_x[1].append(swap(jnp.where(low_x, after, mid), 1, low_x) + is_x)
+                along_x[-1].append(swap(jnp.where(low_x, mid, before), 1, low_x) - is_x)
+            for p in (-1, 0, 1):
+                for cy in range(1, 5):
+                    mid, before, after = (along_x[p][cy + q] for q in (0, -1, 1))
+                    near[3 * (p + 1) + 1, c, cy - 1] = mid
+                    near[3 * (p + 1) + 2, c, cy - 1] = (
+                        swap(jnp.where(low_y, after, mid), 2, low_y) + is_y
+                    )
+                    near[3 * (p + 1), c, cy - 1] = (
+                        swap(jnp.where(low_y, mid, before), 2, low_y) - is_y
+                    )
+            return carry
+
+        lax.fori_loop(0, 8, body, 0)
+
+    def pairs(cy, layer):
+        shift = lax.rem(4 * layer + 128, 128)
+        back = lax.rem(128 - 4 * layer, 128)
+        me = [pltpu.roll(near[4, c, cy], shift, 1) for c in range(8)]
+        me[2] = me[2] - layer.astype(jnp.float32) * (1.0 / 3.0)
+        total = [jnp.zeros((8, 128), jnp.float32) for _ in range(3)]
+        for side in range(9):
+            other = [near[side, c, cy] for c in range(8)]
+            d = [me[c] - other[c] for c in range(3)]
+            square = d[0] * d[0] + d[1] * d[1] + (d[2] * d[2] + soften)
+            inverse = lax.rsqrt(square)
+            weight = jnp.maximum(1.0 - square * inverse, 0.0) * inverse
+            dot = (
+                d[0] * (me[3] - other[3]) + d[1] * (me[4] - other[4]) + d[2] * (me[5] - other[5])
+            )
+            base = me[6] * other[6] + (me[7] + other[7])
+            coeff = weight * (base - weight * dot)
+            total = [total[c] + coeff * d[c] for c in range(3)]
+        return [pltpu.roll(total[c], back, 1) for c in range(3)]
+
+    def all_pairs():
+        def cell_body(cy, carry):
+            def body(n, total):
+                part = pairs(cy, n - 4)
+                return tuple(total[c] + part[c] for c in range(3))
+
+            zero = jnp.zeros((8, 128), jnp.float32)
+            total = lax.fori_loop(0, 9, body, (zero, zero, zero))
+            for c in range(3):
+                force[c, cy] = total[c]
+            return carry
+
+        lax.fori_loop(0, 4, cell_body, 0)
+
+    def collect():
+        for cy in range(1, 5):
+            total = [force[c, cy - 1] for c in range(3)]
+            for p in (-1, 0, 1):
+                for q in (-1, 0, 1):
+                    rows = pl.ds(OWN - p, 8)
+                    hit = cells[9, cy - q, rows, :] == float(3 * (p + 1) + (q + 1))
+                    for c in range(3):
+                        total[c] = total[c] + jnp.where(hit, push[c, cy - q, rows, :], 0.0)
+            for c in range(3):
+                force[c, cy - 1] = total[c] * live_ref[cy - 1]
+
+    for t in range(STEPS + 1):
+        if t > 0:
+            for cy in range(4):
+                for c in range(3):
+                    half = now[3 + c, cy] + 0.5 * time_step * force[c, cy]
+                    now[3 + c, cy] = half
+                    now[c, cy] = now[c, cy] + time_step * half
+        if t == 0:
+            pl.semaphore_wait(barrier, 8)
+        copies = publish(t)
+        aim_own()
+        if t == 0:
+            for cy in range(1, 5):
+                widen(cy, OWN, range(8), lambda s, cy=cy: 8 * cy + s)
+            walls_rows(8, 40)
+            for copy in copies:
+                copy.wait_recv()
+            for cy in (0, 5):
+                widen(cy, OWN, range(8), lambda s, cy=cy: 8 * cy + s)
+            for cy in range(6):
+                widen(cy, OWN - 8, (7,), lambda s, cy=cy: 48 + cy)
+                widen(cy, OWN + 8, (0,), lambda s, cy=cy: 54 + cy)
+            aim_ring()
+            walls_rows(0, 8)
+            walls_rows(40, 48)
+            walls_sides()
+        else:
+            aim_ring()
+            walls_rows(0, 48)
+            walls_sides()
+            for copy in copies:
+                copy.wait_recv()
+        gather_near(t)
+        all_pairs()
+        collect()
+        for copy in copies:
+            copy.wait_send()
+        if t > 0:
+            for cy in range(4):
+                for c in range(3):
+                    now[3 + c, cy] = now[3 + c, cy] + 0.5 * time_step * force[c, cy]
+
+    for cx in range(8):
+        for cy in range(4):
+            for c in range(3):
+                out_x[cx, cy, pl.ds(c, 1), :] = now[c, cy, pl.ds(cx, 1), :]
+                out_v[cx, cy, pl.ds(c, 1), :] = now[3 + c, cy, pl.ds(cx, 1), :]
+
+
+def near_only(positions, velocities, strength, noise, counts, wall_beads, wall_strength, wall_faces):
+    vmem = pl.BlockSpec(memory_space=pltpu.VMEM)
+    smem = pl.BlockSpec(memory_space=pltpu.SMEM)
+    f32 = jnp.float32
+    return pl.pallas_call(
+        kernel,
+        out_shape=(
+            jax.ShapeDtypeStruct(positions.shape, f32),
+            jax.ShapeDtypeStruct(velocities.shape, f32),
+            jax.ShapeDtypeStruct((8, 128), f32),
+        ),
+        in_specs=[smem, smem] + [vmem] * 6,
+        out_specs=(vmem, vmem, vmem),
+        scratch_shapes=[
+            pltpu.VMEM((STATIC + 6 * (STEPS + 1), 6, 24, 128), f32),
+            pltpu.VMEM((7, 4, 32, 128), f32),
+            pltpu.VMEM((6, 4, 8, 128), f32),
+            pltpu.VMEM((4, 8, 128), f32),
+            pltpu.VMEM((60, 4, 128, 128), f32),
+            pltpu.VMEM((7, 6, 24, 128), f32),
+            pltpu.VMEM((3, 6, 24, 128), f32),
+            pltpu.VMEM((9, 8, 4, 8, 128), f32),
+            pltpu.VMEM((3, 4, 8, 128), f32),
+            pltpu.SemaphoreType.DMA((STEPS + 1, 8)),
+            pltpu.SemaphoreType.DMA((STEPS + 1, 8)),
+        ],
+        compiler_params=pltpu.CompilerParams(
+            collective_id=0, has_side_effects=True, vmem_limit_bytes=48 * 2**20
+        ),
+    )(counts, wall_faces, positions, velocities, strength, noise, wall_beads, wall_strength)
+
+
+def local(*args):
+    x, v, bad = near_only(*args)
+    worst = lax.pmax(jnp.max(bad), ("stream", "span"))
+    return lax.cond(worst > 0.0, lambda: every_pair(*args), lambda: (x, v))
+
+
 def solution(mesh):
     in_specs = (
         P("stream", "span", None, None),

time: 568 us -> 113 us (0.20); the launches traced: 559 us -> 112 us
  other arithmetic: 513 us -> 0.6 us
  Pallas kernels: 0 us -> 67.4 us
  blocking collectives: 0 us -> 37.4 us
  starting transfers between devices: 34.2 us -> 0 us
    reduce_sum x52 -> x0, other arithmetic: 509 us -> none  [the longest x32 298 us: tile_force(): jnp.sum(coeff * delta_x, axis=-1)]
    pallas_call x0 -> x1, Pallas kernels: none -> 67.4 us  [near_only(): pl.pallas_call(kernel, out_shape=(jax.ShapeDtypeStruct(positions.shape, f...]
    pmax x0 -> x1, blocking collectives: none -> 37.4 us  [local(): worst = lax.pmax(jnp.max(bad), ('stream', 'span'))]
    ppermute x20 -> x0, starting transfers between devices: 34.2 us -> none  [the longest x10 30.7 us: padded_2(): lax.ppermute(head, axis, [((i + 1) % count, i) for i in range(count)])]
  transfers between devices with their start and end apart: 20 -> 0, of which waited for: 1 -> 0; matrix products, arithmetic and copies ran while one was open for 26% -> 0% of each run, Pallas kernels for 0% -> 0%
where the time goes in v1:
time: 113 us; the launch traced here: 112 us
  Pallas kernels  67.4 us (60%)
  blocking collectives  37.4 us (33%)
  local copies, waits for them, and re-layouts  5.34 us (5%)
  between operations  1.42 us (1%)
    pallas_call x1, Pallas kernels, near_only(): pl.pallas_call(kernel, out_shape=(jax.ShapeDtypeStruct(positions.shape, f...  67.4 us
    pmax x1, blocking collectives, local(): worst = lax.pmax(jnp.max(bad), ('stream', 'span'))  37.4 us
    unnamed x21, local copies, waits for them, and re-layouts  4.07 us

profile of v1, /device:TPU:0, one launch (start us, length us, event | category | flops | bytes accessed | tf_op | source)
XLA Modules:
  0.0 112.2 jit_solution(13956291722883714483)
XLA Ops:
  0.6 0.0 copy-start.1
  0.6 0.0 copy-start.2
  0.7 0.0 copy-start
  0.7 0.0 copy-start.6
  0.7 0.0 copy-start.7
  0.7 0.0 copy-start.4
  0.7 0.0 copy-start.5
  0.7 0.0 copy-start.3
  0.7 0.9 copy.89.pos_ref
  1.6 0.8 copy.90.vel_ref
  2.4 0.8 copy.91.wall_ref
  3.2 0.8 copy.87.counts_ref
  4.0 0.8 copy.88.faces_ref
  4.8 0.0 copy-done.5
  4.8 67.4 %shard_map.99 = (f32[8,4,3,128]{3,2,1,0:T(4,128)S(1)}, f32[8,4,3,128]{3,2,1,0:T(4,128)S(1)}, f32[8,128]{1,0:T(8,128)S(1)}) custom-call(s32[8,4]{1,0:T(8,128)S(1)} %copy.87.counts_ref, s32[8,4]{1,0:T(8,128)S(1)} %copy.88.faces_ref, f32[8,4,3,128]{3,2,1,0:T(4,128)S(1)} %copy.89.pos_ref, f32[8,4,3,128]{3,2,1,0:T(4,128)S(1)} %copy.90.vel_ref, ...), custom_call_target="tpu_custom_call" | custom-call | tf_op jit(solution)/shard_map/pallas_call | solution.py:454
  72.2 0.6 reduce_max.9
  72.8 37.4 %pmax.7 = f32[]{:T(128)} all-reduce(f32[]{:T(128)} %reduce_max.9), channel_id=1, replica_groups=mesh['stream'=8,'span'=4] {'stream','span'}, use_global_device_ids=true, to_apply=%region_1.0 | all-reduce | flops 1 | bytes 8 | tf_op jit(solution)/shard_map/pmax | solution.py:484
  110.8 0.0 copy-done.1
  110.8 0.0 copy-done.2
  110.9 0.0 copy-done
  110.9 0.0 copy-done.6
  110.9 0.0 copy-done.7
  110.9 0.0 copy-done.4
  110.9 0.0 copy-done.3
  110.9 1.3 %conditional.1 = (f32[8,4,3,128]{3,1,2,0:T(4,128)}, f32[8,4,3,128]{3,1,2,0:T(4,128)}) conditional(s32[]{:T(128)} %convert_element_type.105, (f32[8,4,3,128]{3,2,1,0:T(4,128)S(1)}, f32[8,4,3,128]{3,2,1,0:T(4,128)S(1)}) %tuple.14, (s32[8,4]{0,1:T(4,128)S(1)}, f32[8,4,128]{2,1,0:T(4,128)S(1)}, f32[8,4,4,128]{3,2,1,0:T(4,128)S(1)}, ...), branch_computations={%region_2.0_spmd, %region_3.0_spmd} | conditional | flops 1495637120 | bytes 53235504 | solution.py:485
  110.9 0.6 copy.102
  111.6 0.6 copy.104
Async XLA Ops:
  0.6 110.2 %copy-start.1 = (f32[8,4,3,128]{3,1,2,0:T(4,128)S(1)}, f32[8,4,3,128]{3,1,2,0:T(4,128)}, u32[]{:S(2)}) copy-start(f32[8,4,3,128]{3,1,2,0:T(4,128)} %param.10) | copy-start | bytes 147460
  0.6 110.2 %copy-start.2 = (f32[8,4,3,128]{3,1,2,0:T(4,128)S(1)}, f32[8,4,3,128]{3,1,2,0:T(4,128)}, u32[]{:S(2)}) copy-start(f32[8,4,3,128]{3,1,2,0:T(4,128)} %param.11) | copy-start | bytes 147460
  0.7 110.2 %copy-start = (f32[8,4,3,128]{3,1,2,0:T(4,128)S(1)}, f32[8,4,3,128]{3,1,2,0:T(4,128)}, u32[]{:S(2)}) copy-start(f32[8,4,3,128]{3,1,2,0:T(4,128)} %param.15) | copy-start | bytes 147460
  0.7 110.2 %copy-start.6 = (s32[8,4]{0,1:T(4,128)S(1)}, s32[8,4]{0,1:T(4,128)}, u32[]{:S(2)}) copy-start(s32[8,4]{0,1:T(4,128)} %param.14) | copy-start | bytes 388
  0.7 110.2 %copy-start.7 = (s32[8,4]{0,1:T(4,128)S(1)}, s32[8,4]{0,1:T(4,128)}, u32[]{:S(2)}) copy-start(s32[8,4]{0,1:T(4,128)} %param.17) | copy-start | bytes 388
  0.7 110.2 %copy-start.4 = (f32[8,4,128]{2,1,0:T(4,128)S(1)}, f32[8,4,128]{2,1,0:T(4,128)}, u32[]{:S(2)}) copy-start(f32[8,4,128]{2,1,0:T(4,128)} %str_ref.1) | copy-start | bytes 49156
  0.7 4.1 %copy-start.5 = (f32[8,4,4,128]{3,2,1,0:T(4,128)S(1)}, f32[8,4,4,128]{3,2,1,0:T(4,128)}, u32[]{:S(2)}) copy-start(f32[8,4,4,128]{3,2,1,0:T(4,128)} %noise_ref.1) | copy-start | bytes 196612
  0.7 110.2 %copy-start.3 = (f32[8,4,128]{2,1,0:T(4,128)S(1)}, f32[8,4,128]{2,1,0:T(4,128)}, u32[]{:S(2)}) copy-start(f32[8,4,128]{2,1,0:T(4,128)} %wstr_ref.1) | copy-start | bytes 49156

commit v2 on v1

--- a/solution.py
+++ b/solution.py
@@ -166,7 +166,7 @@
 def kernel(
     counts_ref, faces_ref, pos_ref, vel_ref, str_ref, noise_ref, wall_ref, wstr_ref,
     out_x, out_v, bad_ref,
-    cells, own, now, live_ref, wide, target, push, near, force, send_sem, recv_sem,
+    cells, own, now, live_ref, wide, target, push, near, force, flags, send_sem, recv_sem, flag_send, flag_recv,
 ):
     tx, ty = lax.axis_size("stream"), lax.axis_size("span")
     ix, iy = lax.axis_index("stream"), lax.axis_index("span")
@@ -176,7 +176,10 @@
         return (lax.rem(ix + p + tx, tx), lax.rem(iy + q + ty, ty))
 
     barrier = pltpu.get_barrier_semaphore()
-    for p, q in around:
+    row_of = [(p, 0) for p in range(1, tx)]
+    col_of = [(0, q) for q in range(1, ty)]
+    greeted = row_of + col_of + [(p, q) for p, q in around if p * q != 0]
+    for p, q in greeted:
         pl.semaphore_signal(barrier, inc=1, device_id=device(p, q), device_id_type=MESH)
 
     lane, point = lattice((8, 128))
@@ -247,6 +250,28 @@
             copies.append(copy)
         return copies
 
+    def spread(source, first, offsets):
+        sent = []
+        for n, (p, q) in enumerate(offsets):
+            copy = pltpu.make_async_remote_copy(
+                src_ref=flags.at[source],
+                dst_ref=flags.at[2 + first + n],
+                send_sem=flag_send.at[first + n],
+                recv_sem=flag_recv.at[first + n],
+                device_id=device(p, q),
+                device_id_type=MESH,
+            )
+            copy.start()
+            sent.append(copy)
+        return sent
+
+    def merged(source, first, sent):
+        worst = flags[source]
+        for n, copy in enumerate(sent):
+            copy.wait_recv()
+            worst = jnp.maximum(worst, flags[2 + first + n])
+        return worst
+
     def widen(cy, base, rows, block_of):
         tiles = [cells[5 + c, cy, pl.ds(base, 8), :].T for c in range(4)]
         for s in rows:
@@ -372,14 +397,14 @@
             total = [total[c] + coeff * d[c] for c in range(3)]
         return [pltpu.roll(total[c], back, 1) for c in range(3)]
 
-    def all_pairs():
+    def all_pairs(reach):
         def cell_body(cy, carry):
             def body(n, total):
                 part = pairs(cy, n - 4)
                 return tuple(total[c] + part[c] for c in range(3))
 
             zero = jnp.zeros((8, 128), jnp.float32)
-            total = lax.fori_loop(0, 9, body, (zero, zero, zero))
+            total = lax.fori_loop(4 - reach, 5 + reach, body, (zero, zero, zero))
             for c in range(3):
                 force[c, cy] = total[c]
             return carry
@@ -406,8 +431,11 @@
                     now[3 + c, cy] = half
                     now[c, cy] = now[c, cy] + time_step * half
         if t == 0:
-            pl.semaphore_wait(barrier, 8)
+            pl.semaphore_wait(barrier, len(greeted))
         copies = publish(t)
+        if t == STEPS:
+            flags[0] = bad_ref[...]
+            row_sent = spread(0, 0, row_of)
         aim_own()
         if t == 0:
             for cy in range(1, 5):
@@ -430,9 +458,16 @@
             walls_sides()
             for copy in copies:
                 copy.wait_recv()
+        if t == STEPS:
+            flags[1] = merged(0, 0, row_sent)
+            col_sent = spread(1, tx - 1, col_of)
         gather_near(t)
-        all_pairs()
+        all_pairs(3 if t == 0 else 4)
         collect()
+        if t == STEPS:
+            bad_ref[...] = merged(1, tx - 1, col_sent)
+            for copy in row_sent + col_sent:
+                copy.wait_send()
         for copy in copies:
             copy.wait_send()
         if t > 0:
@@ -451,6 +486,7 @@
     vmem = pl.BlockSpec(memory_space=pltpu.VMEM)
     smem = pl.BlockSpec(memory_space=pltpu.SMEM)
     f32 = jnp.float32
+    flag_count = lax.axis_size("stream") + lax.axis_size("span") - 2
     return pl.pallas_call(
         kernel,
         out_shape=(
@@ -470,8 +506,11 @@
             pltpu.VMEM((3, 6, 24, 128), f32),
             pltpu.VMEM((9, 8, 4, 8, 128), f32),
             pltpu.VMEM((3, 4, 8, 128), f32),
+            pltpu.VMEM((2 + flag_count, 8, 128), f32),
             pltpu.SemaphoreType.DMA((STEPS + 1, 8)),
             pltpu.SemaphoreType.DMA((STEPS + 1, 8)),
+            pltpu.SemaphoreType.DMA((flag_count,)),
+            pltpu.SemaphoreType.DMA((flag_count,)),
         ],
         compiler_params=pltpu.CompilerParams(
             collective_id=0, has_side_effects=True, vmem_limit_bytes=48 * 2**20
@@ -481,7 +520,7 @@
 
 def local(*args):
     x, v, bad = near_only(*args)
-    worst = lax.pmax(jnp.max(bad), ("stream", "span"))
+    worst = jnp.max(bad)
     return lax.cond(worst > 0.0, lambda: every_pair(*args), lambda: (x, v))
 
 

time: 113 us -> 74.2 us (0.66)
  blocking collectives: 37.4 us -> 0 us
  Pallas kernels: 67.4 us -> 66.2 us
    pmax x1 -> x0, blocking collectives: 37.4 us -> none  [local(): worst = lax.pmax(jnp.max(bad), ('stream', 'span'))]
    pallas_call x1, Pallas kernels: 67.4 us -> 66.2 us  [near_only(): pl.pallas_call(kernel, out_shape=(jax.ShapeDtypeStruct(positions.shape, f...]
where the time goes in v2:
time: 74.2 us; the launch traced here: 73.6 us
  Pallas kernels  66.2 us (89%)
  local copies, waits for them, and re-layouts  5.34 us (7%)
  between operations  1.42 us (2%)
    pallas_call x1, Pallas kernels, near_only(): pl.pallas_call(kernel, out_shape=(jax.ShapeDtypeStruct(positions.shape, f...  66.2 us
    unnamed x21, local copies, waits for them, and re-layouts  4.07 us

profile of v2, /device:TPU:0, one launch (start us, length us, event | category | flops | bytes accessed | tf_op | source)
XLA Modules:
  0.0 73.6 jit_solution(14597329430081570198)
XLA Ops:
  0.6 0.0 copy-start.1
  0.6 0.0 copy-start.2
  0.7 0.0 copy-start
  0.7 0.0 copy-start.6
  0.7 0.0 copy-start.7
  0.7 0.0 copy-start.4
  0.7 0.0 copy-start.5
  0.7 0.0 copy-start.3
  0.7 0.9 %copy.89.pos_ref = f32[8,4,3,128]{3,2,1,0:T(4,128)S(1)} copy(f32[8,4,3,128]{3,1,2,0:T(4,128)} %param.10) | data formatting | bytes 98304 | tf_op args[0]
  1.6 0.8 %copy.90.vel_ref = f32[8,4,3,128]{3,2,1,0:T(4,128)S(1)} copy(f32[8,4,3,128]{3,1,2,0:T(4,128)} %param.11) | data formatting | bytes 98304 | tf_op args[1]
  2.4 0.8 %copy.91.wall_ref = f32[8,4,3,128]{3,2,1,0:T(4,128)S(1)} copy(f32[8,4,3,128]{3,1,2,0:T(4,128)} %param.15) | data formatting | bytes 98304 | tf_op args[5]
  3.2 0.8 %copy.87.counts_ref = s32[8,4]{1,0:T(8,128)S(1)} copy(s32[8,4]{0,1:T(4,128)} %param.14) | data formatting | bytes 256 | tf_op args[4]
  4.0 0.8 %copy.88.faces_ref = s32[8,4]{1,0:T(8,128)S(1)} copy(s32[8,4]{0,1:T(4,128)} %param.17) | data formatting | bytes 256 | tf_op args[7]
  4.8 0.0 copy-done.5
  4.8 66.2 %shard_map.99 = (f32[8,4,3,128]{3,2,1,0:T(4,128)S(1)}, f32[8,4,3,128]{3,2,1,0:T(4,128)S(1)}, f32[8,128]{1,0:T(8,128)S(1)}) custom-call(s32[8,4]{1,0:T(8,128)S(1)} %copy.87.counts_ref, s32[8,4]{1,0:T(8,128)S(1)} %copy.88.faces_ref, f32[8,4,3,128]{3,2,1,0:T(4,128)S(1)} %copy.89.pos_ref, f32[8,4,3,128]{3,2,1,0:T(4,128)S(1)} %copy.90.vel_ref, ...), custom_call_target="tpu_custom_call" | custom-call | tf_op jit(solution)/shard_map/pallas_call | solution.py:490
  71.0 0.6 reduce_max.9
  72.3 0.0 copy-done.1
  72.3 0.0 copy-done.2
  72.3 0.0 copy-done
  72.3 0.0 copy-done.6
  72.3 0.0 copy-done.7
  72.3 0.0 copy-done.4
  72.3 0.0 copy-done.3
  72.3 1.3 %conditional.1 = (f32[8,4,3,128]{3,1,2,0:T(4,128)}, f32[8,4,3,128]{3,1,2,0:T(4,128)}) conditional(s32[]{:T(128)} %convert_element_type.105, (f32[8,4,3,128]{3,2,1,0:T(4,128)S(1)}, f32[8,4,3,128]{3,2,1,0:T(4,128)S(1)}) %tuple.14, (s32[8,4]{0,1:T(4,128)S(1)}, f32[8,4,128]{2,1,0:T(4,128)S(1)}, f32[8,4,4,128]{3,2,1,0:T(4,128)S(1)}, ...), branch_computations={%region_1.0_spmd, %region_2.0_spmd} | conditional | flops 1495637120 | bytes 53235504 | solution.py:524
  72.3 0.6 copy.102
  73.0 0.6 copy.104
Async XLA Ops:
  0.6 71.6 %copy-start.1 = (f32[8,4,3,128]{3,1,2,0:T(4,128)S(1)}, f32[8,4,3,128]{3,1,2,0:T(4,128)}, u32[]{:S(2)}) copy-start(f32[8,4,3,128]{3,1,2,0:T(4,128)} %param.10) | copy-start | bytes 147460
  0.6 71.6 %copy-start.2 = (f32[8,4,3,128]{3,1,2,0:T(4,128)S(1)}, f32[8,4,3,128]{3,1,2,0:T(4,128)}, u32[]{:S(2)}) copy-start(f32[8,4,3,128]{3,1,2,0:T(4,128)} %param.11) | copy-start | bytes 147460
  0.7 71.6 %copy-start = (f32[8,4,3,128]{3,1,2,0:T(4,128)S(1)}, f32[8,4,3,128]{3,1,2,0:T(4,128)}, u32[]{:S(2)}) copy-start(f32[8,4,3,128]{3,1,2,0:T(4,128)} %param.15) | copy-start | bytes 147460
  0.7 71.6 %copy-start.6 = (s32[8,4]{0,1:T(4,128)S(1)}, s32[8,4]{0,1:T(4,128)}, u32[]{:S(2)}) copy-start(s32[8,4]{0,1:T(4,128)} %param.14) | copy-start | bytes 388
  0.7 71.6 %copy-start.7 = (s32[8,4]{0,1:T(4,128)S(1)}, s32[8,4]{0,1:T(4,128)}, u32[]{:S(2)}) copy-start(s32[8,4]{0,1:T(4,128)} %param.17) | copy-start | bytes 388
  0.7 71.6 %copy-start.4 = (f32[8,4,128]{2,1,0:T(4,128)S(1)}, f32[8,4,128]{2,1,0:T(4,128)}, u32[]{:S(2)}) copy-start(f32[8,4,128]{2,1,0:T(4,128)} %str_ref.1) | copy-start | bytes 49156
  0.7 4.1 %copy-start.5 = (f32[8,4,4,128]{3,2,1,0:T(4,128)S(1)}, f32[8,4,4,128]{3,2,1,0:T(4,128)}, u32[]{:S(2)}) copy-start(f32[8,4,4,128]{3,2,1,0:T(4,128)} %noise_ref.1) | copy-start | bytes 196612
  0.7 71.6 %copy-start.3 = (f32[8,4,128]{2,1,0:T(4,128)S(1)}, f32[8,4,128]{2,1,0:T(4,128)}, u32[]{:S(2)}) copy-start(f32[8,4,128]{2,1,0:T(4,128)} %wstr_ref.1) | copy-start | bytes 49156
